TPU v7x, 256 devices: a whole 4x4x8 slice. The times are simulated.
256 devices in a mesh: sec: 16 (over x, y), op: 16 (over z, core).
Axes of the slice: x: 4, y: 4, z: 8, core: 2. Of those that a mesh axis runs over, the one named last changes fastest.
Arguments:
- wavefunction: bfloat16 [64, 256, 256], P('sec'), may hold values from -6 to 6
- sector_dims: int32 [64, 2], P('sec'), may hold values from 64 to 256, as said below
- term_shift: int32 [176], P('op'), may hold values from -1 to 1
- left_env: bfloat16 [176, 64, 256, 256], P('op', 'sec'), may hold values from -0.02734375 to 0.02734375
- right_env: bfloat16 [176, 64, 256, 256], P('op', 'sec'), may hold values from -0.375 to 0.375
Outputs:
- sigma_blocks: bfloat16 [64, 256, 256], P('sec')
Inputs may be any that keep to these rules, and one draw needn't show every extreme that they name: `sector_dims`: every sector dimension is a multiple of 64.
All inputs are finite; a program needn't handle non-finite values.
Results may differ from a plain program's by a relative error of at most 0.0051.
Values may be sent and summed in bfloat16 or wider, within the bound.
A program may use at most 64 MiB of HBM per device.

v0:
```python
import jax
import jax.numpy as jnp
from jax import lax
from jax.sharding import PartitionSpec as P


def padded(block, sides, width):
    for axis, dim in sides:
        count = lax.axis_size(axis)
        forward = [(i, i + 1) for i in range(count - 1)]
        backward = [(target, source) for source, target in forward]
        low = lax.ppermute(
            lax.slice_in_dim(block, block.shape[dim] - width, None, axis=dim), axis, forward
        )
        high = lax.ppermute(lax.slice_in_dim(block, 0, width, axis=dim), axis, backward)
        block = jnp.concatenate([low, block, high], axis=dim)
    return block


def sector_mask(sector_dims, order):
    positions = jnp.arange(order, dtype=jnp.int32)
    rows_ok = positions[None, :] < sector_dims[:, 0:1]
    cols_ok = positions[None, :] < sector_dims[:, 1:2]
    return rows_ok[:, :, None] & cols_ok[:, None, :]


def body(wavefunction, sector_dims, term_shift, left_env, right_env):
    local_count = wavefunction.shape[0]
    order = wavefunction.shape[1]
    keep = sector_mask(sector_dims, order)
    masked = jnp.where(keep, wavefunction, jnp.zeros_like(wavefunction))
    widened = padded(masked, (("sec", 0),), 1)
    picks = jnp.arange(local_count, dtype=jnp.int32)[None, :] + term_shift[:, None] + 1
    source = jnp.take(widened, picks, axis=0)
    first = jnp.einsum(
        "kjab,kjbc->kjac", left_env, source, preferred_element_type=jnp.float32
    ).astype(jnp.bfloat16)
    partial_sum = jnp.einsum("kjac,kjdc->jad", first, right_env, preferred_element_type=jnp.float32)
    total = lax.psum(partial_sum, "op")
    return jnp.where(keep, total, jnp.zeros_like(total)).astype(jnp.bfloat16)


def solution(mesh):
    return jax.shard_map(
        body,
        mesh=mesh,
        in_specs=(
            P("sec", None, None),
            P("sec", None),
            P("op"),
            P("op", "sec", None, None),
            P("op", "sec", None, None),
        ),
        out_specs=P("sec", None, None),
        check_vma=False,
    )
```

profile of v0, /device:TPU:24, one launch (start us, length us, event | category | flops | bytes accessed | tf_op | source)
XLA Modules:
  0.0 88.5 jit_solution(9762345111098702933)
XLA Ops:
  0.0 0.8 slice_bitcast_fusion.1
  0.8 0.1 iota_compare_fusion
  0.8 1.3 %and_select_fusion.1 = bf16[4,256,256]{2,1,0:T(8,128)(2,1)S(1)} fusion(bf16[4,256,256]{2,1,0:T(8,128)(2,1)} %param.5, pred[4,256]{1,0:T(4,128)(4,1)S(1)} %get-tuple-element.9, pred[4,256]{1,0:T(4,128)(4,1)S(1)} %get-tuple-element.10), kind=kLoop, calls=%fused_computation.11 | loop fusion | flops 524288 | bytes 1050624 | tf_op jit(solution)/shard_map/jit(_where)/select_n | solution.py:31
  2.2 3.1 %collective-permute-start = (bf16[1,256,256]{2,1,0:T(8,128)(2,1)S(1)}, bf16[1,256,256]{2,1,0:T(8,128)(2,1)S(1)}, u32[]{:S(2)}, u32[]{:S(2)}) collective-permute-start(bf16[1,256,256]{2,1,0:T(8,128)(2,1)S(1)} %get-tuple-element.5), channel_id=1, source_target_pairs={{0,16},{16,32},{32,48},{48,64},{64,80},{80,96},{96,112},{112,128},... | collective-permute-start | bytes 393224 | tf_op jit(solution)/shard_map/ppermute | solution.py:12
  5.2 2.8 %collective-permute-start.1 = (bf16[1,256,256]{2,1,0:T(8,128)(2,1)S(1)}, bf16[1,256,256]{2,1,0:T(8,128)(2,1)S(1)}, u32[]{:S(2)}, u32[]{:S(2)}) collective-permute-start(bf16[1,256,256]{2,1,0:T(8,128)(2,1)S(1)} %get-tuple-element.6), channel_id=1, source_target_pairs={{16,0},{32,16},{48,32},{64,48},{80,64},{96,80},{112,96},{128,112},... | collective-permute-start | bytes 393224 | tf_op jit(solution)/shard_map/ppermute | solution.py:15
  8.0 0.7 compare_select_fusion
  8.7 0.7 fusion.27
  9.5 0.1 reshape.101
  9.6 0.0 collective-permute-done
  9.6 4.6 %collective-permute-done.1 = bf16[1,256,256]{2,1,0:T(8,128)(2,1)S(1)} collective-permute-done((bf16[1,256,256]{2,1,0:T(8,128)(2,1)S(1)}, bf16[1,256,256]{2,1,0:T(8,128)(2,1)S(1)}, u32[]{:S(2)}, u32[]{:S(2)}) %collective-permute-start.1) | collective-permute-done | bytes 131104 | tf_op jit(solution)/shard_map/ppermute | solution.py:15
  14.2 0.1 pad_maximum_fusion
  14.3 4.8 %gather_fusion = bf16[44,256,256]{2,1,0:T(8,128)(2,1)} fusion(bf16[6,256,256]{2,1,0:T(8,128)(2,1)S(1)} %pad_maximum_fusion, s32[1024]{0:T(1024)S(1)} %pad_clamp_fusion), kind=kCustom, calls=%fused_computation | custom fusion | bytes 11534512 | tf_op jit(solution)/shard_map/jit(_take)/gather | solution.py:34
  19.1 7.8 %fusion.15 = f32[4,256,256]{2,1,0:T(8,128)S(1)} fusion(bf16[11,4,256,256]{3,2,1,0:T(8,128)(2,1)} %param.9, bf16[11,4,256,256]{3,2,1,0:T(8,128)(2,1)} %param.8, bf16[11,4,256,256]{3,2,1,0:T(8,128)(2,1)} %bitcast.15, pred[11,4]{1,0:T(8,128)(4,1)S(1)} %fusion.27), kind=kOutput, calls=%fused_computation.9 | convolution fusion | flops 2958557184 | bytes 18350124 | tf_op jit(solution)/shard_map/kjac,kjdc->jad/dot_general | solution.py:38
  26.8 60.6 %all-reduce.1 = bf16[4,256,256]{2,1,0:T(8,128)(2,1)S(1)} all-reduce(f32[4,256,256]{2,1,0:T(8,128)S(1)} %fusion.15), channel_id=1, replica_groups=mesh['sec'=16,'op'=16] {'op'}, use_global_device_ids=true, to_apply=%region_0.1 | all-reduce | flops 262144 | bytes 1572864 | tf_op jit(solution)/shard_map/psum | solution.py:39
  87.5 1.0 %fusion.24 = bf16[4,256,256]{2,1,0:T(8,128)(2,1)} fusion(bf16[4,256,256]{2,1,0:T(8,128)(2,1)S(1)} %all-reduce.1, pred[4,256]{1,0:T(4,128)(4,1)S(1)} %get-tuple-element.9, pred[4,256]{1,0:T(4,128)(4,1)S(1)} %get-tuple-element.10), kind=kLoop, calls=%fused_computation.12 | loop fusion | flops 524288 | bytes 1050624 | tf_op jit(solution)/shard_map/convert_element_type | solution.py:40
  (2 shorter events, 0.0 us)
Async XLA Ops:
  2.2 7.4 %collective-permute-start = (bf16[1,256,256]{2,1,0:T(8,128)(2,1)S(1)}, bf16[1,256,256]{2,1,0:T(8,128)(2,1)S(1)}, u32[]{:S(2)}, u32[]{:S(2)}) collective-permute-start(bf16[1,256,256]{2,1,0:T(8,128)(2,1)S(1)} %get-tuple-element.5), channel_id=1, source_target_pairs={{0,16},{16,32},{32,48},{48,64},{64,80},{80,96},{96,112},{112,128},... | collective-permute-start | bytes 393224 | tf_op jit(solution)/shard_map/ppermute | solution.py:12
  5.2 9.0 %collective-permute-start.1 = (bf16[1,256,256]{2,1,0:T(8,128)(2,1)S(1)}, bf16[1,256,256]{2,1,0:T(8,128)(2,1)S(1)}, u32[]{:S(2)}, u32[]{:S(2)}) collective-permute-start(bf16[1,256,256]{2,1,0:T(8,128)(2,1)S(1)} %get-tuple-element.6), channel_id=1, source_target_pairs={{16,0},{32,16},{48,32},{64,48},{80,64},{96,80},{112,96},{128,112},... | collective-permute-start | bytes 393224 | tf_op jit(solution)/shard_map/ppermute | solution.py:15
where the time goes:
time: 88.8 us; the launch traced here: 88.5 us
  blocking collectives  60.6 us (68%)
  matrix products  7.78 us (9%)
  starting transfers between devices  5.84 us (7%)
  local copies, waits for them, and re-layouts  5.62 us (6%)
  waiting for transfers between devices  4.62 us (5%)
  other arithmetic  3.98 us (4%)
    psum x1, blocking collectives, body(): total = lax.psum(partial_sum, 'op')  60.6 us
    dot_general x1, matrix products, body(): jnp.einsum('kjac,kjdc->jad', first, right_env, preferred_element_type=jnp...  7.78 us
    gather x1, local copies, waits for them, and re-layouts, body(): source = jnp.take(widened, picks, axis=0)  4.76 us
    ppermute x1, waiting for transfers between devices, padded(): lax.ppermute(lax.slice_in_dim(block, 0, width, axis=dim), axis, backward)  4.62 us
    ppermute x1, starting transfers between devices, padded(): lax.ppermute(lax.slice_in_dim(block, block.shape[dim] - width, None, axis...  3.06 us
    ppermute x1, starting transfers between devices, padded(): lax.ppermute(lax.slice_in_dim(block, 0, width, axis=dim), axis, backward)  2.78 us
  transfers between devices with their start and end apart: 2, of which 1 were waited for; matrix products, arithmetic and copies ran while one was open for 2% of the time, Pallas kernels for 0%

commit v1 on v0

v1 whole, which is shorter than its diff:
```python
import functools

import jax
import jax.numpy as jnp
from jax import lax
from jax.experimental import pallas as pl
from jax.experimental.pallas import tpu as pltpu
from jax.sharding import PartitionSpec as P

MESH = pl.DeviceIdType.MESH
NT = (((1,), (1,)), ((), ()))


def kernel(
    nsec,
    nz,
    dims_ref,
    shift_ref,
    wave_ref,
    left_ref,
    right_ref,
    out_ref,
    wide,
    near,
    left,
    right,
    part,
    sib,
    packed,
    landed,
    wave_sem,
    left_sem,
    right_sem,
    halo_send,
    halo_recv,
    sib_send,
    sib_recv,
    rs_send,
    rs_recv,
    ag_send,
    ag_recv,
    fin_send,
    fin_recv,
):
    order = wide.shape[1]
    terms = left.shape[1]
    rows = order // nz
    sec = lax.axis_index("sec")
    me = lax.axis_index("op")
    z = lax.div(me, 2)
    c = lax.rem(me, 2)

    def peer(d):
        return {"op": lax.rem(z + d, nz) * 2 + c}

    sibling = {"op": z * 2 + 1 - c}

    def beside(d):
        return {"sec": lax.rem(sec + d + nsec, nsec)}

    def sector_of(p, e):
        return 1 - p + e * (1 + 2 * p)

    def load(it):
        s = sector_of(it // 2, c if it % 2 else 1 - c)
        return (
            pltpu.make_async_copy(left_ref.at[:, s], left.at[it], left_sem.at[it]),
            pltpu.make_async_copy(right_ref.at[:, s], right.at[it], right_sem.at[it]),
        )

    def load_wave(s):
        return pltpu.make_async_copy(wave_ref.at[s], wide.at[s + 1], wave_sem.at[s])

    for s in (0, 3, 1, 2):
        load_wave(s).start()
    for it in range(4):
        for copy in load(it):
            copy.start()

    barrier = pltpu.get_barrier_semaphore()
    for d in range(1, nz):
        pl.semaphore_signal(barrier, inc=1, device_id=peer(d), device_id_type=MESH)
    pl.semaphore_signal(barrier, inc=1, device_id=sibling, device_id_type=MESH)
    for d in (-1, 1):
        pl.semaphore_signal(barrier, inc=1, device_id=beside(d), device_id_type=MESH)

    def mask(s):
        row = lax.broadcasted_iota(jnp.int32, (order, order), 0)
        col = lax.broadcasted_iota(jnp.int32, (order, order), 1)
        keep = (row < dims_ref[s, 0]) & (col < dims_ref[s, 1])
        block = wide[s + 1].astype(jnp.float32)
        wide[s + 1] = jnp.where(keep, block, 0.0).astype(jnp.bfloat16)

    for s in (0, 3):
        load_wave(s).wait()
        mask(s)
    pl.semaphore_wait(barrier, nz + 2)

    def halo(i):
        e = c if i == 0 else 1 - c
        return pltpu.make_async_remote_copy(
            src_ref=wide.at[1 + 3 * e],
            dst_ref=wide.at[5 - 5 * e],
            send_sem=halo_send.at[i],
            recv_sem=halo_recv.at[i],
            device_id=beside(2 * e - 1),
            device_id_type=MESH,
        )

    for i in range(2):
        halo(i).start()
    for s in (1, 2):
        load_wave(s).wait()
        mask(s)

    def to_sibling(p):
        return pltpu.make_async_remote_copy(
            src_ref=part.at[2 * p],
            dst_ref=sib.at[p],
            send_sem=sib_send.at[p],
            recv_sem=sib_recv.at[p],
            device_id=sibling,
            device_id_type=MESH,
        )

    def scatter(p, d):
        chunk = lax.rem(z + d, nz) * rows
        return pltpu.make_async_remote_copy(
            src_ref=packed.at[p, pl.ds(pl.multiple_of(chunk, rows), rows)],
            dst_ref=landed.at[p, d - 1],
            send_sem=rs_send.at[p, d - 1],
            recv_sem=rs_recv.at[p, d - 1],
            device_id=peer(d),
            device_id_type=MESH,
        )

    mine = pl.ds(pl.multiple_of(z * rows, rows), rows)

    def gather(p, d):
        own = sector_of(p, c)
        return pltpu.make_async_remote_copy(
            src_ref=out_ref.at[own, mine],
            dst_ref=out_ref.at[own, mine],
            send_sem=ag_send.at[p, d - 1],
            recv_sem=ag_recv.at[p, d - 1],
            device_id=peer(d),
            device_id_type=MESH,
        )

    def final(p):
        own = sector_of(p, c)
        return pltpu.make_async_remote_copy(
            src_ref=out_ref.at[own],
            dst_ref=out_ref.at[own],
            send_sem=fin_send.at[p],
            recv_sem=fin_recv.at[p],
            device_id=sibling,
            device_id_type=MESH,
        )

    far = sorted(range(1, nz), key=lambda d: -min(d, nz - d))

    def step(it, carry):
        p = lax.div(it, 2)
        q = lax.rem(it, 2)
        e = q * c + (1 - q) * (1 - c)
        s = sector_of(p, e)
        for i in range(2):

            @pl.when(it == 2 + i)
            def _():
                halo(i).wait_recv()
                f = c if i == 0 else 1 - c

                @pl.when(sec == (nsec - 1) * (1 - f))
                def _():
                    wide[5 - 5 * f] = jnp.zeros((order, order), jnp.bfloat16)

        for n in range(3):
            near[n] = wide[s + n]
        pltpu.make_async_copy(left_ref.at[:, s], left.at[it], left_sem.at[it]).wait()
        pltpu.make_async_copy(right_ref.at[:, s], right.at[it], right_sem.at[it]).wait()
        total = None
        for k in range(terms):
            first = jnp.dot(
                left[it, k], near[shift_ref[k] + 1], preferred_element_type=jnp.float32
            ).astype(jnp.bfloat16)
            term = lax.dot_general(first, right[it, k], NT, preferred_element_type=jnp.float32)
            total = term if total is None else total + term
        part[it] = total
        for p_now in range(2):

            @pl.when(it == 2 * p_now)
            def _():
                to_sibling(p_now).start()

            @pl.when(it == 2 * p_now + 1)
            def _():
                to_sibling(p_now).wait_recv()
                packed[p_now] = (part[2 * p_now + 1] + sib[p_now]).astype(jnp.bfloat16)
                for d in far:
                    scatter(p_now, d).start()

        return carry

    lax.fori_loop(0, 4, step, 0)

    for p in range(2):
        total = part[2 * p + 1, mine] + sib[p, mine]
        for d in range(1, nz):
            scatter(p, d).wait_recv()
            total += landed[p, d - 1].astype(jnp.float32)
        out_ref[sector_of(p, c), mine] = total.astype(jnp.bfloat16)
        for d in far:
            gather(p, d).start()
    for p in range(2):
        for d in range(1, nz):
            gather(p, d).wait_recv()
        final(p).start()
    for i in range(2):
        halo(i).wait_send()
        to_sibling(i).wait_send()
        for d in range(1, nz):
            scatter(i, d).wait_send()
            gather(i, d).wait_send()
    for p in range(2):
        final(p).wait()


def body(nsec, nz, wavefunction, sector_dims, term_shift, left_env, right_env):
    count, order, _ = wavefunction.shape
    terms = left_env.shape[0]
    rows = order // nz
    bf16, f32 = jnp.bfloat16, jnp.float32
    dma = pltpu.SemaphoreType.DMA
    smem = pl.BlockSpec(memory_space=pltpu.SMEM)
    anywhere = pl.BlockSpec(memory_space=pl.ANY)
    total = pl.pallas_call(
        functools.partial(kernel, nsec, nz),
        out_shape=pltpu.VMEM((count, order, order), bf16),
        in_specs=[smem, smem, anywhere, anywhere, anywhere],
        out_specs=pl.BlockSpec(memory_space=pltpu.VMEM),
        scratch_shapes=[
            pltpu.VMEM((count + 2, order, order), bf16),
            pltpu.VMEM((3, order, order), bf16),
            pltpu.VMEM((count, terms, order, order), bf16),
            pltpu.VMEM((count, terms, order, order), bf16),
            pltpu.VMEM((count, order, order), f32),
            pltpu.VMEM((2, order, order), f32),
            pltpu.VMEM((2, order, order), bf16),
            pltpu.VMEM((2, nz - 1, rows, order), bf16),
            dma((count,)),
            dma((count,)),
            dma((count,)),
            dma((2,)),
            dma((2,)),
            dma((2,)),
            dma((2,)),
            dma((2, nz - 1)),
            dma((2, nz - 1)),
            dma((2, nz - 1)),
            dma((2, nz - 1)),
            dma((2,)),
            dma((2,)),
        ],
        compiler_params=pltpu.CompilerParams(
            collective_id=0, has_side_effects=True, vmem_limit_bytes=32 << 20
        ),
    )(sector_dims, term_shift, wavefunction, left_env, right_env)
    positions = jnp.arange(order, dtype=jnp.int32)
    rows_ok = positions[None, :] < sector_dims[:, 0:1]
    cols_ok = positions[None, :] < sector_dims[:, 1:2]
    keep = rows_ok[:, :, None] & cols_ok[:, None, :]
    return jnp.where(keep, total, jnp.zeros_like(total))


def solution(mesh):
    nsec, nop = mesh.shape["sec"], mesh.shape["op"]
    return jax.shard_map(
        functools.partial(body, nsec, nop // 2),
        mesh=mesh,
        in_specs=(
            P("sec", None, None),
            P("sec", None),
            P("op"),
            P("op", "sec", None, None),
            P("op", "sec", None, None),
        ),
        out_specs=P("sec", None, None),
        check_vma=False,
    )
```

time: 88.8 us -> 42.3 us (0.48)
  the two profiles are of different devices: /device:TPU:24 before, /device:TPU:1 now
where the time goes in v1:
time: 42.3 us; the launch traced here: 42.1 us
  Pallas kernels  33.2 us (78%)
  local copies, waits for them, and re-layouts  7.74 us (18%)
  other arithmetic  1.12 us (3%)
    pallas_call x1, Pallas kernels, body(): pl.pallas_call(functools.partial(kernel, nsec, nz), out_shape=pltpu.VMEM(...  33.2 us
    unnamed x11, local copies, waits for them, and re-layouts  7.73 us
    select_n x1, other arithmetic, body(): return jnp.where(keep, total, jnp.zeros_like(total))  1.05 us

profile of v1, /device:TPU:1, one launch (start us, length us, event | category | flops | bytes accessed | tf_op | source)
XLA Modules:
  0.0 42.1 jit_solution(15809152206104923071)
XLA Ops:
  0.0 0.8 %copy.6.dims_ref = s32[4,2]{1,0:T(4,128)S(1)} copy(s32[4,2]{0,1:T(2,128)} %param.6) | data formatting | bytes 64 | tf_op args[1]
  0.8 0.0 copy-start
  0.8 2.6 %copy-done = bf16[11,4,256,256]{3,2,1,0:T(8,128)(2,1)S(1)} copy-done((bf16[11,4,256,256]{3,2,1,0:T(8,128)(2,1)S(1)}, bf16[11,4,256,256]{3,2,1,0:T(8,128)(2,1)}, u32[]{:S(2)}) %copy-start) | copy-done | bytes 5767192
  3.4 0.0 copy-start.1
  3.4 2.6 %copy-done.1 = bf16[11,4,256,256]{3,2,1,0:T(8,128)(2,1)S(1)} copy-done((bf16[11,4,256,256]{3,2,1,0:T(8,128)(2,1)S(1)}, bf16[11,4,256,256]{3,2,1,0:T(8,128)(2,1)}, u32[]{:S(2)}) %copy-start.1) | copy-done | bytes 5767192
  6.0 0.0 copy-start.2
  6.0 1.0 %copy-done.2 = bf16[4,256,256]{2,1,0:T(8,128)(2,1)S(1)} copy-done((bf16[4,256,256]{2,1,0:T(8,128)(2,1)S(1)}, bf16[4,256,256]{2,1,0:T(8,128)(2,1)}, u32[]{:S(2)}) %copy-start.2) | copy-done | bytes 524312
  7.1 0.0 copy-start.3
  7.1 0.7 %copy-done.3 = s32[11]{0:T(128)S(1)} copy-done((s32[11]{0:T(128)S(1)}, s32[11]{0:T(128)}, u32[]{:S(2)}) %copy-start.3) | copy-done | bytes 68
  7.7 0.0 copy-start.4
  7.7 33.2 %shard_map.55 = bf16[4,256,256]{2,1,0:T(8,128)(2,1)S(1)} custom-call(s32[4,2]{1,0:T(4,128)S(1)} %copy.6.dims_ref, s32[11]{0:T(128)S(1)} %copy-done.3, bf16[4,256,256]{2,1,0:T(8,128)(2,1)S(1)} %copy-done.2, bf16[11,4,256,256]{3,2,1,0:T(8,128)(2,1)S(1)} %copy-done, bf16[11,4,256,256]{3,2,1,0:T(8,128)(2,1)S(1)} %copy-done.1), custom_call_target="tpu_custom_call" | custom-call | tf_op jit(solution)/shard_map/pallas_call | solution.py:238
  41.0 0.0 copy-done.4
  41.0 0.1 iota_compare_fusion
  41.1 1.0 %and_select_fusion = bf16[4,256,256]{2,1,0:T(8,128)(2,1)} fusion(bf16[4,256,256]{2,1,0:T(8,128)(2,1)S(1)} %shard_map.55, pred[4,256]{1,0:T(4,128)(4,1)S(1)} %get-tuple-element.7, pred[4,256]{1,0:T(4,128)(4,1)S(1)} %get-tuple-element.8), kind=kLoop, calls=%fused_computation | loop fusion | flops 524288 | bytes 1050624 | tf_op jit(solution)/shard_map/jit(_where)/select_n | solution.py:274
  (1 shorter events, 0.0 us)
Async XLA Ops:
  0.8 2.6 %copy-start = (bf16[11,4,256,256]{3,2,1,0:T(8,128)(2,1)S(1)}, bf16[11,4,256,256]{3,2,1,0:T(8,128)(2,1)}, u32[]{:S(2)}) copy-start(bf16[11,4,256,256]{3,2,1,0:T(8,128)(2,1)} %left_ref.1) | copy-start | bytes 17301508
  3.4 2.6 %copy-start.1 = (bf16[11,4,256,256]{3,2,1,0:T(8,128)(2,1)S(1)}, bf16[11,4,256,256]{3,2,1,0:T(8,128)(2,1)}, u32[]{:S(2)}) copy-start(bf16[11,4,256,256]{3,2,1,0:T(8,128)(2,1)} %right_ref.1) | copy-start | bytes 17301508
  6.0 1.0 %copy-start.2 = (bf16[4,256,256]{2,1,0:T(8,128)(2,1)S(1)}, bf16[4,256,256]{2,1,0:T(8,128)(2,1)}, u32[]{:S(2)}) copy-start(bf16[4,256,256]{2,1,0:T(8,128)(2,1)} %wave_ref.1) | copy-start | bytes 1572868
  7.1 0.7 %copy-start.3 = (s32[11]{0:T(128)S(1)}, s32[11]{0:T(128)}, u32[]{:S(2)}) copy-start(s32[11]{0:T(128)} %shift_ref.1) | copy-start | bytes 136
  7.7 33.2 %copy-start.4 = (s32[4,2]{0,1:T(2,128)S(1)}, s32[4,2]{0,1:T(2,128)}, u32[]{:S(2)}) copy-start(s32[4,2]{0,1:T(2,128)} %param.6) | copy-start | bytes 100

commit v2 on v1

--- a/solution.py
+++ b/solution.py
@@ -14,8 +14,8 @@
 def kernel(
     nsec,
     nz,
-    dims_ref,
-    shift_ref,
+    dims_hbm,
+    shift_hbm,
     wave_ref,
     left_ref,
     right_ref,
@@ -28,6 +28,9 @@
     sib,
     packed,
     landed,
+    dims_ref,
+    shift_ref,
+    small_sem,
     wave_sem,
     left_sem,
     right_sem,
@@ -71,8 +74,12 @@
     def load_wave(s):
         return pltpu.make_async_copy(wave_ref.at[s], wide.at[s + 1], wave_sem.at[s])
 
+    load_dims = pltpu.make_async_copy(dims_hbm, dims_ref, small_sem.at[0])
+    load_shift = pltpu.make_async_copy(shift_hbm, shift_ref, small_sem.at[1])
+    load_dims.start()
     for s in (0, 3, 1, 2):
         load_wave(s).start()
+    load_shift.start()
     for it in range(4):
         for copy in load(it):
             copy.start()
@@ -84,13 +91,16 @@
     for d in (-1, 1):
         pl.semaphore_signal(barrier, inc=1, device_id=beside(d), device_id_type=MESH)
 
+    def masked(block, s, start):
+        row = lax.broadcasted_iota(jnp.int32, block.shape, 0) + start
+        col = lax.broadcasted_iota(jnp.int32, block.shape, 1)
+        keep = (row < dims_ref[0, s]) & (col < dims_ref[1, s])
+        return jnp.where(keep, block, 0.0).astype(jnp.bfloat16)
+
     def mask(s):
-        row = lax.broadcasted_iota(jnp.int32, (order, order), 0)
-        col = lax.broadcasted_iota(jnp.int32, (order, order), 1)
-        keep = (row < dims_ref[s, 0]) & (col < dims_ref[s, 1])
-        block = wide[s + 1].astype(jnp.float32)
-        wide[s + 1] = jnp.where(keep, block, 0.0).astype(jnp.bfloat16)
-
+        wide[s + 1] = masked(wide[s + 1].astype(jnp.float32), s, 0)
+
+    load_dims.wait()
     for s in (0, 3):
         load_wave(s).wait()
         mask(s)
@@ -112,6 +122,8 @@
     for s in (1, 2):
         load_wave(s).wait()
         mask(s)
+
+    load_shift.wait()
 
     def to_sibling(p):
         return pltpu.make_async_remote_copy(
@@ -210,7 +222,8 @@
         for d in range(1, nz):
             scatter(p, d).wait_recv()
             total += landed[p, d - 1].astype(jnp.float32)
-        out_ref[sector_of(p, c), mine] = total.astype(jnp.bfloat16)
+        own = sector_of(p, c)
+        out_ref[own, mine] = masked(total, own, z * rows)
         for d in far:
             gather(p, d).start()
     for p in range(2):
@@ -233,12 +246,11 @@
     rows = order // nz
     bf16, f32 = jnp.bfloat16, jnp.float32
     dma = pltpu.SemaphoreType.DMA
-    smem = pl.BlockSpec(memory_space=pltpu.SMEM)
-    anywhere = pl.BlockSpec(memory_space=pl.ANY)
-    total = pl.pallas_call(
+    hbm = pl.BlockSpec(memory_space=pltpu.HBM)
+    return pl.pallas_call(
         functools.partial(kernel, nsec, nz),
         out_shape=pltpu.VMEM((count, order, order), bf16),
-        in_specs=[smem, smem, anywhere, anywhere, anywhere],
+        in_specs=[hbm] * 5,
         out_specs=pl.BlockSpec(memory_space=pltpu.VMEM),
         scratch_shapes=[
             pltpu.VMEM((count + 2, order, order), bf16),
@@ -249,6 +261,9 @@
             pltpu.VMEM((2, order, order), f32),
             pltpu.VMEM((2, order, order), bf16),
             pltpu.VMEM((2, nz - 1, rows, order), bf16),
+            pltpu.SMEM((2, count), jnp.int32),
+            pltpu.SMEM((terms,), jnp.int32),
+            dma((2,)),
             dma((count,)),
             dma((count,)),
             dma((count,)),
@@ -266,12 +281,10 @@
         compiler_params=pltpu.CompilerParams(
             collective_id=0, has_side_effects=True, vmem_limit_bytes=32 << 20
         ),
-    )(sector_dims, term_shift, wavefunction, left_env, right_env)
-    positions = jnp.arange(order, dtype=jnp.int32)
-    rows_ok = positions[None, :] < sector_dims[:, 0:1]
-    cols_ok = positions[None, :] < sector_dims[:, 1:2]
-    keep = rows_ok[:, :, None] & cols_ok[:, None, :]
-    return jnp.where(keep, total, jnp.zeros_like(total))
+    )(*(
+        pltpu.with_memory_space_constraint(x, pltpu.HBM)
+        for x in (sector_dims.T, term_shift, wavefunction, left_env, right_env)
+    ))
 
 
 def solution(mesh):

time: 42.3 us -> 32.2 us (0.76)
  local copies, waits for them, and re-layouts: 7.74 us -> 0.8 us
  Pallas kernels: 33.2 us -> 31.3 us
  other arithmetic: 1.12 us -> 0 us
    unnamed x11 -> x1, local copies, waits for them, and re-layouts: 7.73 us -> 0.8 us
    pallas_call x1, Pallas kernels: 33.2 us -> 31.3 us  [body(): pl.pallas_call(functools.partial(kernel, nsec, nz), out_shape=pltpu.VMEM(...]
    select_n x1 -> x0, other arithmetic: 1.05 us -> none  [body(): return jnp.where(keep, total, jnp.zeros_like(total))]
where the time goes in v2:
time: 32.2 us; the launch traced here: 32.1 us
  Pallas kernels  31.3 us (97%)
  local copies, waits for them, and re-layouts  0.8 us (2%)
    pallas_call x1, Pallas kernels, body(): pl.pallas_call(functools.partial(kernel, nsec, nz), out_shape=pltpu.VMEM(...  31.3 us
    unnamed x1, local copies, waits for them, and re-layouts  0.8 us

profile of v2, /device:TPU:1, one launch (start us, length us, event | category | flops | bytes accessed | tf_op | source)
XLA Modules:
  0.0 32.1 jit_solution(16028012841311088405)
XLA Ops:
  0.0 31.3 %shard_map.55 = bf16[4,256,256]{2,1,0:T(8,128)(2,1)S(1)} custom-call(s32[2,4]{1,0:T(2,128)} %bitcast.1, s32[11]{0:T(128)} %shift_hbm.1, bf16[4,256,256]{2,1,0:T(8,128)(2,1)} %wave_ref.1, bf16[11,4,256,256]{3,2,1,0:T(8,128)(2,1)} %left_ref.1, bf16[11,4,256,256]{3,2,1,0:T(8,128)(2,1)} %right_ref.1), custom_call_target="tpu_custom_call" | custom-call | tf_op jit(solution)/shard_map/pallas_call | solution.py:250
  31.3 0.8 %copy.7 = bf16[4,256,256]{2,1,0:T(8,128)(2,1)} copy(bf16[4,256,256]{2,1,0:T(8,128)(2,1)S(1)} %shard_map.55) | data formatting | bytes 1048576

commit v3 on v2

--- a/solution.py
+++ b/solution.py
@@ -44,6 +44,7 @@
     ag_recv,
     fin_send,
     fin_recv,
+    ready,
 ):
     order = wide.shape[1]
     terms = left.shape[1]
@@ -57,6 +58,7 @@
         return {"op": lax.rem(z + d, nz) * 2 + c}
 
     sibling = {"op": z * 2 + 1 - c}
+    near_z = (1, 2, nz - 2, nz - 1)
 
     def beside(d):
         return {"sec": lax.rem(sec + d + nsec, nsec)}
@@ -65,7 +67,8 @@
         return 1 - p + e * (1 + 2 * p)
 
     def load(it):
-        s = sector_of(it // 2, c if it % 2 else 1 - c)
+        q = lax.rem(it, 2)
+        s = sector_of(lax.div(it, 2), q * c + (1 - q) * (1 - c))
         return (
             pltpu.make_async_copy(left_ref.at[:, s], left.at[it], left_sem.at[it]),
             pltpu.make_async_copy(right_ref.at[:, s], right.at[it], right_sem.at[it]),
@@ -77,19 +80,17 @@
     load_dims = pltpu.make_async_copy(dims_hbm, dims_ref, small_sem.at[0])
     load_shift = pltpu.make_async_copy(shift_hbm, shift_ref, small_sem.at[1])
     load_dims.start()
-    for s in (0, 3, 1, 2):
+    waves = (3 * c, 3 - 3 * c, 1, 2)
+    for s in waves:
         load_wave(s).start()
     load_shift.start()
-    for it in range(4):
-        for copy in load(it):
-            copy.start()
+    for copy in load(0):
+        copy.start()
 
     barrier = pltpu.get_barrier_semaphore()
-    for d in range(1, nz):
-        pl.semaphore_signal(barrier, inc=1, device_id=peer(d), device_id_type=MESH)
-    pl.semaphore_signal(barrier, inc=1, device_id=sibling, device_id_type=MESH)
-    for d in (-1, 1):
-        pl.semaphore_signal(barrier, inc=1, device_id=beside(d), device_id_type=MESH)
+    greeted = [beside(-1), beside(1), sibling] + [peer(d) for d in near_z]
+    for device in greeted:
+        pl.semaphore_signal(barrier, inc=1, device_id=device, device_id_type=MESH)
 
     def masked(block, s, start):
         row = lax.broadcasted_iota(jnp.int32, block.shape, 0) + start
@@ -101,28 +102,35 @@
         wide[s + 1] = masked(wide[s + 1].astype(jnp.float32), s, 0)
 
     load_dims.wait()
-    for s in (0, 3):
+    load_wave(waves[0]).wait()
+    mask(waves[0])
+    pl.semaphore_wait(barrier, len(greeted))
+
+    halo = pltpu.make_async_remote_copy(
+        src_ref=wide.at[1 + 3 * c],
+        dst_ref=wide.at[5 - 5 * c],
+        send_sem=halo_send.at[0],
+        recv_sem=halo_recv.at[0],
+        device_id=beside(2 * c - 1),
+        device_id_type=MESH,
+    )
+    halo.start()
+    for d in (2, nz - 2):
+        pl.semaphore_signal(ready, inc=1, device_id=peer(d), device_id_type=MESH)
+
+    def passed(slot):
+        return pltpu.make_async_remote_copy(
+            src_ref=wide.at[slot],
+            dst_ref=wide.at[slot],
+            send_sem=halo_send.at[1],
+            recv_sem=halo_recv.at[1],
+            device_id=sibling,
+            device_id_type=MESH,
+        )
+
+    for s in waves[1:]:
         load_wave(s).wait()
         mask(s)
-    pl.semaphore_wait(barrier, nz + 2)
-
-    def halo(i):
-        e = c if i == 0 else 1 - c
-        return pltpu.make_async_remote_copy(
-            src_ref=wide.at[1 + 3 * e],
-            dst_ref=wide.at[5 - 5 * e],
-            send_sem=halo_send.at[i],
-            recv_sem=halo_recv.at[i],
-            device_id=beside(2 * e - 1),
-            device_id_type=MESH,
-        )
-
-    for i in range(2):
-        halo(i).start()
-    for s in (1, 2):
-        load_wave(s).wait()
-        mask(s)
-
     load_shift.wait()
 
     def to_sibling(p):
@@ -177,47 +185,67 @@
         q = lax.rem(it, 2)
         e = q * c + (1 - q) * (1 - c)
         s = sector_of(p, e)
-        for i in range(2):
-
-            @pl.when(it == 2 + i)
+
+        @pl.when(it == 2)
+        def _():
+            halo.wait_recv()
+
+            @pl.when(sec == (nsec - 1) * (1 - c))
             def _():
-                halo(i).wait_recv()
-                f = c if i == 0 else 1 - c
-
-                @pl.when(sec == (nsec - 1) * (1 - f))
-                def _():
-                    wide[5 - 5 * f] = jnp.zeros((order, order), jnp.bfloat16)
+                wide[5 - 5 * c] = jnp.zeros((order, order), jnp.bfloat16)
+
+            passed(5 - 5 * c).start()
+
+        @pl.when(it == 3)
+        def _():
+            passed(5 * c).wait_recv()
 
         for n in range(3):
             near[n] = wide[s + n]
-        pltpu.make_async_copy(left_ref.at[:, s], left.at[it], left_sem.at[it]).wait()
-        pltpu.make_async_copy(right_ref.at[:, s], right.at[it], right_sem.at[it]).wait()
-        total = None
-        for k in range(terms):
-            first = jnp.dot(
+        left_now, right_now = load(it)
+
+        @pl.when(it == 0)
+        def _():
+            for later in range(1, 4):
+                for copy in load(later):
+                    copy.start()
+
+        left_now.wait()
+        right_now.wait()
+
+        def first(k):
+            return jnp.dot(
                 left[it, k], near[shift_ref[k] + 1], preferred_element_type=jnp.float32
             ).astype(jnp.bfloat16)
-            term = lax.dot_general(first, right[it, k], NT, preferred_element_type=jnp.float32)
+
+        total, ahead = None, first(0)
+        for k in range(terms):
+            now, ahead = ahead, first(k + 1) if k + 1 < terms else None
+            term = lax.dot_general(now, right[it, k], NT, preferred_element_type=jnp.float32)
             total = term if total is None else total + term
         part[it] = total
-        for p_now in range(2):
-
-            @pl.when(it == 2 * p_now)
+
+        @pl.when(q == 0)
+        def _():
+            to_sibling(p).start()
+
+        @pl.when(q == 1)
+        def _():
+            to_sibling(p).wait_recv()
+            packed[p] = (total + sib[p]).astype(jnp.bfloat16)
+
+            @pl.when(p == 0)
             def _():
-                to_sibling(p_now).start()
-
-            @pl.when(it == 2 * p_now + 1)
-            def _():
-                to_sibling(p_now).wait_recv()
-                packed[p_now] = (part[2 * p_now + 1] + sib[p_now]).astype(jnp.bfloat16)
-                for d in far:
-                    scatter(p_now, d).start()
+                pl.semaphore_wait(ready, 2)
+
+            for d in far:
+                scatter(p, d).start()
 
         return carry
 
     lax.fori_loop(0, 4, step, 0)
 
-    for p in range(2):
+    def reduce(p, carry):
         total = part[2 * p + 1, mine] + sib[p, mine]
         for d in range(1, nz):
             scatter(p, d).wait_recv()
@@ -226,18 +254,27 @@
         out_ref[own, mine] = masked(total, own, z * rows)
         for d in far:
             gather(p, d).start()
-    for p in range(2):
+        return carry
+
+    def spread(p, carry):
         for d in range(1, nz):
             gather(p, d).wait_recv()
         final(p).start()
-    for i in range(2):
-        halo(i).wait_send()
-        to_sibling(i).wait_send()
+        return carry
+
+    def finish(p, carry):
+        to_sibling(p).wait_send()
         for d in range(1, nz):
-            scatter(i, d).wait_send()
-            gather(i, d).wait_send()
-    for p in range(2):
+            scatter(p, d).wait_send()
+            gather(p, d).wait_send()
         final(p).wait()
+        return carry
+
+    lax.fori_loop(0, 2, reduce, 0)
+    lax.fori_loop(0, 2, spread, 0)
+    lax.fori_loop(0, 2, finish, 0)
+    halo.wait_send()
+    passed(5 - 5 * c).wait_send()
 
 
 def body(nsec, nz, wavefunction, sector_dims, term_shift, left_env, right_env):
@@ -277,6 +314,7 @@
             dma((2, nz - 1)),
             dma((2,)),
             dma((2,)),
+            pltpu.SemaphoreType.REGULAR,
         ],
         compiler_params=pltpu.CompilerParams(
             collective_id=0, has_side_effects=True, vmem_limit_bytes=32 << 20

time: 32.2 us -> 30.8 us (0.957)
  Pallas kernels: 31.3 us -> 30 us
    pallas_call x1, Pallas kernels: 31.3 us -> 30 us  [body(): pl.pallas_call(functools.partial(kernel, nsec, nz), out_shape=pltpu.VMEM(...]
where the time goes in v3:
time: 30.8 us
  Pallas kernels  30 us (97%)
  local copies, waits for them, and re-layouts  0.8 us (3%)
    pallas_call x1, Pallas kernels, body(): pl.pallas_call(functools.partial(kernel, nsec, nz), out_shape=pltpu.VMEM(...  30 us
    unnamed x1, local copies, waits for them, and re-layouts  0.8 us

profile of v3, /device:TPU:1, one launch (start us, length us, event | category | flops | bytes accessed | tf_op | source)
XLA Modules:
  0.0 30.8 jit_solution(15535035219177787610)
XLA Ops:
  0.0 30.0 %shard_map.55 = bf16[4,256,256]{2,1,0:T(8,128)(2,1)S(1)} custom-call(s32[2,4]{1,0:T(2,128)} %bitcast.1, s32[11]{0:T(128)} %shift_hbm.1, bf16[4,256,256]{2,1,0:T(8,128)(2,1)} %wave_ref.1, bf16[11,4,256,256]{3,2,1,0:T(8,128)(2,1)} %left_ref.1, bf16[11,4,256,256]{3,2,1,0:T(8,128)(2,1)} %right_ref.1), custom_call_target="tpu_custom_call" | custom-call | tf_op jit(solution)/shard_map/pallas_call | solution.py:287
  30.0 0.8 %copy.7 = bf16[4,256,256]{2,1,0:T(8,128)(2,1)} copy(bf16[4,256,256]{2,1,0:T(8,128)(2,1)S(1)} %shard_map.55) | data formatting | bytes 1048576

commit v4 on v3

--- a/solution.py
+++ b/solution.py
@@ -28,6 +28,7 @@
     sib,
     packed,
     landed,
+    done,
     dims_ref,
     shift_ref,
     small_sem,
@@ -42,8 +43,8 @@
     rs_recv,
     ag_send,
     ag_recv,
-    fin_send,
-    fin_recv,
+    share_send,
+    share_recv,
     ready,
 ):
     order = wide.shape[1]
@@ -55,13 +56,13 @@
     c = lax.rem(me, 2)
 
     def peer(d):
-        return {"op": lax.rem(z + d, nz) * 2 + c}
+        return {"op": lax.rem(z + d, nz) * 2 + 1}
 
     sibling = {"op": z * 2 + 1 - c}
     near_z = (1, 2, nz - 2, nz - 1)
 
-    def beside(d):
-        return {"sec": lax.rem(sec + d + nsec, nsec)}
+    def beside(d, core):
+        return {"sec": lax.rem(sec + d + nsec, nsec), "op": z * 2 + core}
 
     def sector_of(p, e):
         return 1 - p + e * (1 + 2 * p)
@@ -80,17 +81,29 @@
     load_dims = pltpu.make_async_copy(dims_hbm, dims_ref, small_sem.at[0])
     load_shift = pltpu.make_async_copy(shift_hbm, shift_ref, small_sem.at[1])
     load_dims.start()
-    waves = (3 * c, 3 - 3 * c, 1, 2)
-    for s in waves:
+    for s in (3, 0, 1, 2):
         load_wave(s).start()
     load_shift.start()
     for copy in load(0):
         copy.start()
 
     barrier = pltpu.get_barrier_semaphore()
-    greeted = [beside(-1), beside(1), sibling] + [peer(d) for d in near_z]
-    for device in greeted:
-        pl.semaphore_signal(barrier, inc=1, device_id=device, device_id_type=MESH)
+
+    def signal(sem, device):
+        pl.semaphore_signal(sem, inc=1, device_id=device, device_id_type=MESH)
+
+    signal(barrier, sibling)
+
+    @pl.when(c == 1)
+    def _():
+        signal(barrier, beside(-1, 1))
+        for d in near_z:
+            signal(barrier, peer(d))
+            signal(barrier, {"op": lax.rem(z + d, nz) * 2})
+
+    @pl.when(c == 0)
+    def _():
+        signal(barrier, beside(1, 1))
 
     def masked(block, s, start):
         row = lax.broadcasted_iota(jnp.int32, block.shape, 0) + start
@@ -102,33 +115,39 @@
         wide[s + 1] = masked(wide[s + 1].astype(jnp.float32), s, 0)
 
     load_dims.wait()
-    load_wave(waves[0]).wait()
-    mask(waves[0])
-    pl.semaphore_wait(barrier, len(greeted))
-
-    halo = pltpu.make_async_remote_copy(
-        src_ref=wide.at[1 + 3 * c],
-        dst_ref=wide.at[5 - 5 * c],
-        send_sem=halo_send.at[0],
-        recv_sem=halo_recv.at[0],
-        device_id=beside(2 * c - 1),
-        device_id_type=MESH,
-    )
-    halo.start()
-    for d in (2, nz - 2):
-        pl.semaphore_signal(ready, inc=1, device_id=peer(d), device_id_type=MESH)
+    for s in (3, 0):
+        load_wave(s).wait()
+        mask(s)
+    pl.semaphore_wait(barrier, 5 + 2 * c)
+
+    def halo(i):
+        return pltpu.make_async_remote_copy(
+            src_ref=wide.at[4 - 3 * i],
+            dst_ref=wide.at[5 * i],
+            send_sem=halo_send.at[i],
+            recv_sem=halo_recv.at[0],
+            device_id=beside(1 - 2 * i, 1 - i),
+            device_id_type=MESH,
+        )
+
+    @pl.when(c == 1)
+    def _():
+        for i in (1, 0):
+            halo(i).start()
+        for d in (2, nz - 2):
+            signal(ready, peer(d))
 
     def passed(slot):
         return pltpu.make_async_remote_copy(
             src_ref=wide.at[slot],
             dst_ref=wide.at[slot],
-            send_sem=halo_send.at[1],
+            send_sem=halo_send.at[2],
             recv_sem=halo_recv.at[1],
             device_id=sibling,
             device_id_type=MESH,
         )
 
-    for s in waves[1:]:
+    for s in (1, 2):
         load_wave(s).wait()
         mask(s)
     load_shift.wait()
@@ -147,36 +166,48 @@
         chunk = lax.rem(z + d, nz) * rows
         return pltpu.make_async_remote_copy(
             src_ref=packed.at[p, pl.ds(pl.multiple_of(chunk, rows), rows)],
-            dst_ref=landed.at[p, d - 1],
-            send_sem=rs_send.at[p, d - 1],
-            recv_sem=rs_recv.at[p, d - 1],
+            dst_ref=landed.at[p, c * (nz - 1) + d - 1],
+            send_sem=rs_send.at[p],
+            recv_sem=rs_recv.at[p],
             device_id=peer(d),
             device_id_type=MESH,
         )
 
     mine = pl.ds(pl.multiple_of(z * rows, rows), rows)
 
+    def hand_over(p):
+        return pltpu.make_async_remote_copy(
+            src_ref=packed.at[p, mine],
+            dst_ref=landed.at[p, 2 * (nz - 1)],
+            send_sem=rs_send.at[p],
+            recv_sem=rs_recv.at[p],
+            device_id=sibling,
+            device_id_type=MESH,
+        )
+
     def gather(p, d):
-        own = sector_of(p, c)
-        return pltpu.make_async_remote_copy(
-            src_ref=out_ref.at[own, mine],
-            dst_ref=out_ref.at[own, mine],
-            send_sem=ag_send.at[p, d - 1],
+        return pltpu.make_async_remote_copy(
+            src_ref=done.at[p, z],
+            dst_ref=done.at[p, z],
+            send_sem=ag_send.at[p],
             recv_sem=ag_recv.at[p, d - 1],
             device_id=peer(d),
             device_id_type=MESH,
         )
 
-    def final(p):
-        own = sector_of(p, c)
-        return pltpu.make_async_remote_copy(
-            src_ref=out_ref.at[own],
-            dst_ref=out_ref.at[own],
-            send_sem=fin_send.at[p],
-            recv_sem=fin_recv.at[p],
+    def share(p, d):
+        chunk = lax.rem(z - d + nz, nz)
+        return pltpu.make_async_remote_copy(
+            src_ref=done.at[p, chunk],
+            dst_ref=done.at[p, chunk],
+            send_sem=share_send.at[p],
+            recv_sem=share_recv.at[p],
             device_id=sibling,
             device_id_type=MESH,
         )
+
+    def wait_all(ref, sem):
+        pltpu.make_async_copy(ref, ref, sem).wait()
 
     far = sorted(range(1, nz), key=lambda d: -min(d, nz - d))
 
@@ -188,7 +219,7 @@
 
         @pl.when(it == 2)
         def _():
-            halo.wait_recv()
+            halo(1 - c).wait_recv()
 
             @pl.when(sec == (nsec - 1) * (1 - c))
             def _():
@@ -236,45 +267,79 @@
 
             @pl.when(p == 0)
             def _():
-                pl.semaphore_wait(ready, 2)
+                pl.semaphore_wait(ready, 1 + c)
+
+                @pl.when(c == 1)
+                def _():
+                    signal(ready, sibling)
 
             for d in far:
                 scatter(p, d).start()
 
+            @pl.when(c == 0)
+            def _():
+                hand_over(p).start()
+
         return carry
 
     lax.fori_loop(0, 4, step, 0)
 
     def reduce(p, carry):
-        total = part[2 * p + 1, mine] + sib[p, mine]
+        mine_now = part[2 * p + 1, mine] + sib[p, mine]
+        wait_all(landed.at[p], rs_recv.at[p])
+        sums = [landed[p, 2 * (nz - 1)].astype(jnp.float32), mine_now]
         for d in range(1, nz):
-            scatter(p, d).wait_recv()
-            total += landed[p, d - 1].astype(jnp.float32)
-        own = sector_of(p, c)
-        out_ref[own, mine] = masked(total, own, z * rows)
+            for core in range(2):
+                sums[core] += landed[p, core * (nz - 1) + d - 1].astype(jnp.float32)
+        for core in range(2):
+            done[p, z, core] = masked(sums[core], sector_of(p, core), z * rows)
         for d in far:
             gather(p, d).start()
+        share(p, 0).start()
         return carry
 
-    def spread(p, carry):
-        for d in range(1, nz):
+    def pass_on(p, carry):
+        for d in reversed(far):
             gather(p, d).wait_recv()
-        final(p).start()
+            share(p, d).start()
         return carry
+
+    def place(p):
+        for core in range(2):
+            for n in range(nz):
+                out_ref[sector_of(p, core), pl.ds(n * rows, rows)] = done[p, n, core]
+
+    @pl.when(c == 1)
+    def _():
+        lax.fori_loop(0, 2, reduce, 0)
+        lax.fori_loop(0, 2, pass_on, 0)
 
     def finish(p, carry):
         to_sibling(p).wait_send()
-        for d in range(1, nz):
-            scatter(p, d).wait_send()
-            gather(p, d).wait_send()
-        final(p).wait()
+
+        @pl.when(c == 0)
+        def _():
+            wait_all(packed.at[p], rs_send.at[p])
+            wait_all(done.at[p], share_recv.at[p])
+
+        place(p)
+
+        @pl.when(c == 1)
+        def _():
+            wait_all(landed.at[p, pl.ds(0, nz - 1)], rs_send.at[p])
+            wait_all(done.at[p, pl.ds(0, nz - 1)], ag_send.at[p])
+            wait_all(done.at[p], share_send.at[p])
+
         return carry
 
-    lax.fori_loop(0, 2, reduce, 0)
-    lax.fori_loop(0, 2, spread, 0)
+    passed(5 - 5 * c).wait_send()
+
+    @pl.when(c == 1)
+    def _():
+        for i in range(2):
+            halo(i).wait_send()
+
     lax.fori_loop(0, 2, finish, 0)
-    halo.wait_send()
-    passed(5 - 5 * c).wait_send()
 
 
 def body(nsec, nz, wavefunction, sector_dims, term_shift, left_env, right_env):
@@ -297,20 +362,21 @@
             pltpu.VMEM((count, order, order), f32),
             pltpu.VMEM((2, order, order), f32),
             pltpu.VMEM((2, order, order), bf16),
-            pltpu.VMEM((2, nz - 1, rows, order), bf16),
+            pltpu.VMEM((2, 2 * nz - 1, rows, order), bf16),
+            pltpu.VMEM((2, nz, 2, rows, order), bf16),
             pltpu.SMEM((2, count), jnp.int32),
             pltpu.SMEM((terms,), jnp.int32),
             dma((2,)),
             dma((count,)),
             dma((count,)),
             dma((count,)),
-            dma((2,)),
-            dma((2,)),
-            dma((2,)),
-            dma((2,)),
-            dma((2, nz - 1)),
-            dma((2, nz - 1)),
-            dma((2, nz - 1)),
+            dma((3,)),
+            dma((2,)),
+            dma((2,)),
+            dma((2,)),
+            dma((2,)),
+            dma((2,)),
+            dma((2,)),
             dma((2, nz - 1)),
             dma((2,)),
             dma((2,)),

time: 30.8 us -> 29.4 us (0.955)
  Pallas kernels: 30 us -> 28.5 us
    pallas_call x1, Pallas kernels: 30 us -> 28.5 us  [body(): pl.pallas_call(functools.partial(kernel, nsec, nz), out_shape=pltpu.VMEM(...]
where the time goes in v4:
time: 29.4 us; the launch traced here: 29.3 us
  Pallas kernels  28.5 us (97%)
  local copies, waits for them, and re-layouts  0.8 us (3%)
    pallas_call x1, Pallas kernels, body(): pl.pallas_call(functools.partial(kernel, nsec, nz), out_shape=pltpu.VMEM(...  28.5 us
    unnamed x1, local copies, waits for them, and re-layouts  0.8 us

profile of v4, /device:TPU:1, one launch (start us, length us, event | category | flops | bytes accessed | tf_op | source)
XLA Modules:
  0.0 29.3 jit_solution(254368104249756357)
XLA Ops:
  0.0 28.5 %shard_map.55 = bf16[4,256,256]{2,1,0:T(8,128)(2,1)S(1)} custom-call(s32[2,4]{1,0:T(2,128)} %bitcast.1, s32[11]{0:T(128)} %shift_hbm.1, bf16[4,256,256]{2,1,0:T(8,128)(2,1)} %wave_ref.1, bf16[11,4,256,256]{3,2,1,0:T(8,128)(2,1)} %left_ref.1, bf16[11,4,256,256]{3,2,1,0:T(8,128)(2,1)} %right_ref.1), custom_call_target="tpu_custom_call" | custom-call | tf_op jit(solution)/shard_map/pallas_call | solution.py:352
  28.5 0.8 %copy.7 = bf16[4,256,256]{2,1,0:T(8,128)(2,1)} copy(bf16[4,256,256]{2,1,0:T(8,128)(2,1)S(1)} %shard_map.55) | data formatting | bytes 1048576

commit v5 on v4

--- a/solution.py
+++ b/solution.py
@@ -64,6 +64,9 @@
     def beside(d, core):
         return {"sec": lax.rem(sec + d + nsec, nsec), "op": z * 2 + core}
 
+    before = lax.div(sec + nsec - 1, nsec)
+    after = lax.div(2 * nsec - 2 - sec, nsec)
+
     def sector_of(p, e):
         return 1 - p + e * (1 + 2 * p)
 
@@ -96,12 +99,15 @@
 
     @pl.when(c == 1)
     def _():
-        signal(barrier, beside(-1, 1))
+        @pl.when(before == 1)
+        def _():
+            signal(barrier, beside(-1, 1))
+
         for d in near_z:
             signal(barrier, peer(d))
             signal(barrier, {"op": lax.rem(z + d, nz) * 2})
 
-    @pl.when(c == 0)
+    @pl.when((c == 0) & (after == 1))
     def _():
         signal(barrier, beside(1, 1))
 
@@ -118,7 +124,7 @@
     for s in (3, 0):
         load_wave(s).wait()
         mask(s)
-    pl.semaphore_wait(barrier, 5 + 2 * c)
+    pl.semaphore_wait(barrier, 5 + c * (before + after))
 
     def halo(i):
         return pltpu.make_async_remote_copy(
@@ -132,8 +138,14 @@
 
     @pl.when(c == 1)
     def _():
-        for i in (1, 0):
-            halo(i).start()
+        @pl.when(before == 1)
+        def _():
+            halo(1).start()
+
+        @pl.when(after == 1)
+        def _():
+            halo(0).start()
+
         for d in (2, nz - 2):
             signal(ready, peer(d))
 
@@ -219,9 +231,11 @@
 
         @pl.when(it == 2)
         def _():
-            halo(1 - c).wait_recv()
-
-            @pl.when(sec == (nsec - 1) * (1 - c))
+            @pl.when(c * before + (1 - c) * after == 1)
+            def _():
+                halo(1 - c).wait_recv()
+
+            @pl.when(c * before + (1 - c) * after == 0)
             def _():
                 wide[5 - 5 * c] = jnp.zeros((order, order), jnp.bfloat16)
 
@@ -334,10 +348,13 @@
 
     passed(5 - 5 * c).wait_send()
 
-    @pl.when(c == 1)
-    def _():
-        for i in range(2):
-            halo(i).wait_send()
+    @pl.when((c == 1) & (before == 1))
+    def _():
+        halo(1).wait_send()
+
+    @pl.when((c == 1) & (after == 1))
+    def _():
+        halo(0).wait_send()
 
     lax.fori_loop(0, 2, finish, 0)
 

time: 29.4 us -> 26.6 us (0.905); the launches traced: 29.3 us -> 26.2 us
  Pallas kernels: 28.5 us -> 25.4 us
    pallas_call x1, Pallas kernels: 28.5 us -> 25.4 us  [body(): pl.pallas_call(functools.partial(kernel, nsec, nz), out_shape=pltpu.VMEM(...]
where the time goes in v5:
time: 26.6 us; the launch traced here: 26.2 us
  Pallas kernels  25.4 us (95%)
  local copies, waits for them, and re-layouts  0.8 us (3%)
    pallas_call x1, Pallas kernels, body(): pl.pallas_call(functools.partial(kernel, nsec, nz), out_shape=pltpu.VMEM(...  25.4 us
    unnamed x1, local copies, waits for them, and re-layouts  0.8 us

profile of v5, /device:TPU:1, one launch (start us, length us, event | category | flops | bytes accessed | tf_op | source)
XLA Modules:
  0.0 26.2 jit_solution(1593807259049637312)
XLA Ops:
  0.0 25.4 %shard_map.55 = bf16[4,256,256]{2,1,0:T(8,128)(2,1)S(1)} custom-call(s32[2,4]{1,0:T(2,128)} %bitcast.1, s32[11]{0:T(128)} %shift_hbm.1, bf16[4,256,256]{2,1,0:T(8,128)(2,1)} %wave_ref.1, bf16[11,4,256,256]{3,2,1,0:T(8,128)(2,1)} %left_ref.1, bf16[11,4,256,256]{3,2,1,0:T(8,128)(2,1)} %right_ref.1), custom_call_target="tpu_custom_call" | custom-call | tf_op jit(solution)/shard_map/pallas_call | solution.py:369
  25.4 0.8 %copy.7 = bf16[4,256,256]{2,1,0:T(8,128)(2,1)} copy(bf16[4,256,256]{2,1,0:T(8,128)(2,1)S(1)} %shard_map.55) | data formatting | bytes 1048576

commit v6 on v5

--- a/solution.py
+++ b/solution.py
@@ -9,6 +9,7 @@
 
 MESH = pl.DeviceIdType.MESH
 NT = (((1,), (1,)), ((), ()))
+ROW = 4
 
 
 def kernel(
@@ -25,6 +26,7 @@
     left,
     right,
     part,
+    lent,
     sib,
     packed,
     landed,
@@ -59,7 +61,7 @@
         return {"op": lax.rem(z + d, nz) * 2 + 1}
 
     sibling = {"op": z * 2 + 1 - c}
-    near_z = (1, 2, nz - 2, nz - 1)
+    far = sorted(range(1, nz), key=lambda d: -min(d, nz - d))
 
     def beside(d, core):
         return {"sec": lax.rem(sec + d + nsec, nsec), "op": z * 2 + core}
@@ -67,8 +69,16 @@
     before = lax.div(sec + nsec - 1, nsec)
     after = lax.div(2 * nsec - 2 - sec, nsec)
 
+    def turned(at):
+        return lax.div(lax.rem(at, ROW) + 1, ROW)
+
+    def role(e, turn):
+        return e + turn - 2 * e * turn
+
+    r = role(c, turned(sec))
+
     def sector_of(p, e):
-        return 1 - p + e * (1 + 2 * p)
+        return (1 - p) * (1 + e) + 3 * p * role(e, turned(sec))
 
     def load(it):
         q = lax.rem(it, 2)
@@ -80,6 +90,26 @@
 
     def load_wave(s):
         return pltpu.make_async_copy(wave_ref.at[s], wide.at[s + 1], wave_sem.at[s])
+
+    barrier = pltpu.get_barrier_semaphore()
+
+    def signal(sem, device):
+        pl.semaphore_signal(sem, inc=1, device_id=device, device_id_type=MESH)
+
+    @pl.when((r == 1) & (before == 1))
+    def _():
+        signal(barrier, beside(-1, 1))
+
+    @pl.when((r == 0) & (after == 1))
+    def _():
+        signal(barrier, beside(1, 1))
+
+    signal(barrier, sibling)
+
+    @pl.when(c == 1)
+    def _():
+        for d in far:
+            signal(barrier, {"op": lax.rem(z + d, nz) * 2})
 
     load_dims = pltpu.make_async_copy(dims_hbm, dims_ref, small_sem.at[0])
     load_shift = pltpu.make_async_copy(shift_hbm, shift_ref, small_sem.at[1])
@@ -90,27 +120,6 @@
     for copy in load(0):
         copy.start()
 
-    barrier = pltpu.get_barrier_semaphore()
-
-    def signal(sem, device):
-        pl.semaphore_signal(sem, inc=1, device_id=device, device_id_type=MESH)
-
-    signal(barrier, sibling)
-
-    @pl.when(c == 1)
-    def _():
-        @pl.when(before == 1)
-        def _():
-            signal(barrier, beside(-1, 1))
-
-        for d in near_z:
-            signal(barrier, peer(d))
-            signal(barrier, {"op": lax.rem(z + d, nz) * 2})
-
-    @pl.when((c == 0) & (after == 1))
-    def _():
-        signal(barrier, beside(1, 1))
-
     def masked(block, s, start):
         row = lax.broadcasted_iota(jnp.int32, block.shape, 0) + start
         col = lax.broadcasted_iota(jnp.int32, block.shape, 1)
@@ -124,7 +133,6 @@
     for s in (3, 0):
         load_wave(s).wait()
         mask(s)
-    pl.semaphore_wait(barrier, 5 + c * (before + after))
 
     def halo(i):
         return pltpu.make_async_remote_copy(
@@ -132,12 +140,14 @@
             dst_ref=wide.at[5 * i],
             send_sem=halo_send.at[i],
             recv_sem=halo_recv.at[0],
-            device_id=beside(1 - 2 * i, 1 - i),
+            device_id=beside(1 - 2 * i, role(1 - i, turned(sec + 1 - 2 * i + nsec))),
             device_id_type=MESH,
         )
 
     @pl.when(c == 1)
     def _():
+        pl.semaphore_wait(barrier, 1 + before + after)
+
         @pl.when(before == 1)
         def _():
             halo(1).start()
@@ -145,9 +155,6 @@
         @pl.when(after == 1)
         def _():
             halo(0).start()
-
-        for d in (2, nz - 2):
-            signal(ready, peer(d))
 
     def passed(slot):
         return pltpu.make_async_remote_copy(
@@ -166,7 +173,7 @@
 
     def to_sibling(p):
         return pltpu.make_async_remote_copy(
-            src_ref=part.at[2 * p],
+            src_ref=lent.at[p],
             dst_ref=sib.at[p],
             send_sem=sib_send.at[p],
             recv_sem=sib_recv.at[p],
@@ -221,8 +228,6 @@
     def wait_all(ref, sem):
         pltpu.make_async_copy(ref, ref, sem).wait()
 
-    far = sorted(range(1, nz), key=lambda d: -min(d, nz - d))
-
     def step(it, carry):
         p = lax.div(it, 2)
         q = lax.rem(it, 2)
@@ -231,19 +236,19 @@
 
         @pl.when(it == 2)
         def _():
-            @pl.when(c * before + (1 - c) * after == 1)
+            @pl.when(r * before + (1 - r) * after == 1)
             def _():
-                halo(1 - c).wait_recv()
-
-            @pl.when(c * before + (1 - c) * after == 0)
+                halo(1 - r).wait_recv()
+
+            @pl.when(r * before + (1 - r) * after == 0)
             def _():
-                wide[5 - 5 * c] = jnp.zeros((order, order), jnp.bfloat16)
-
-            passed(5 - 5 * c).start()
+                wide[5 - 5 * r] = jnp.zeros((order, order), jnp.bfloat16)
+
+            passed(5 - 5 * r).start()
 
         @pl.when(it == 3)
         def _():
-            passed(5 * c).wait_recv()
+            passed(5 * r).wait_recv()
 
         for n in range(3):
             near[n] = wide[s + n]
@@ -268,24 +273,27 @@
             now, ahead = ahead, first(k + 1) if k + 1 < terms else None
             term = lax.dot_general(now, right[it, k], NT, preferred_element_type=jnp.float32)
             total = term if total is None else total + term
-        part[it] = total
+
+        @pl.when((it == 0) & (c == 0))
+        def _():
+            pl.semaphore_wait(barrier, nz)
+            signal(ready, sibling)
 
         @pl.when(q == 0)
         def _():
+            lent[p] = total.astype(jnp.bfloat16)
             to_sibling(p).start()
 
         @pl.when(q == 1)
         def _():
             to_sibling(p).wait_recv()
-            packed[p] = (total + sib[p]).astype(jnp.bfloat16)
-
-            @pl.when(p == 0)
+            both = total + sib[p].astype(jnp.float32)
+            part[p] = both
+            packed[p] = both.astype(jnp.bfloat16)
+
+            @pl.when((p == 0) & (c == 1))
             def _():
-                pl.semaphore_wait(ready, 1 + c)
-
-                @pl.when(c == 1)
-                def _():
-                    signal(ready, sibling)
+                pl.semaphore_wait(ready, 1)
 
             for d in far:
                 scatter(p, d).start()
@@ -299,7 +307,7 @@
     lax.fori_loop(0, 4, step, 0)
 
     def reduce(p, carry):
-        mine_now = part[2 * p + 1, mine] + sib[p, mine]
+        mine_now = part[p, mine]
         wait_all(landed.at[p], rs_recv.at[p])
         sums = [landed[p, 2 * (nz - 1)].astype(jnp.float32), mine_now]
         for d in range(1, nz):
@@ -346,7 +354,7 @@
 
         return carry
 
-    passed(5 - 5 * c).wait_send()
+    passed(5 - 5 * r).wait_send()
 
     @pl.when((c == 1) & (before == 1))
     def _():
@@ -376,8 +384,9 @@
             pltpu.VMEM((3, order, order), bf16),
             pltpu.VMEM((count, terms, order, order), bf16),
             pltpu.VMEM((count, terms, order, order), bf16),
-            pltpu.VMEM((count, order, order), f32),
             pltpu.VMEM((2, order, order), f32),
+            pltpu.VMEM((2, order, order), bf16),
+            pltpu.VMEM((2, order, order), bf16),
             pltpu.VMEM((2, order, order), bf16),
             pltpu.VMEM((2, 2 * nz - 1, rows, order), bf16),
             pltpu.VMEM((2, nz, 2, rows, order), bf16),

time: 26.6 us -> 26.5 us (level)
  the two profiles are of different devices: /device:TPU:1 before, /device:TPU:7 now
where the time goes in v6:
time: 26.5 us; the launch traced here: 26.4 us
  Pallas kernels  25.6 us (97%)
  local copies, waits for them, and re-layouts  0.8 us (3%)
    pallas_call x1, Pallas kernels, body(): pl.pallas_call(functools.partial(kernel, nsec, nz), out_shape=pltpu.VMEM(...  25.6 us
    unnamed x1, local copies, waits for them, and re-layouts  0.8 us

profile of v6, /device:TPU:7, one launch (start us, length us, event | category | flops | bytes accessed | tf_op | source)
XLA Modules:
  0.0 26.4 jit_solution(14265313567036348433)
XLA Ops:
  0.0 25.6 %shard_map.55 = bf16[4,256,256]{2,1,0:T(8,128)(2,1)S(1)} custom-call(s32[2,4]{1,0:T(2,128)} %bitcast.1, s32[11]{0:T(128)} %shift_hbm.1, bf16[4,256,256]{2,1,0:T(8,128)(2,1)} %wave_ref.1, bf16[11,4,256,256]{3,2,1,0:T(8,128)(2,1)} %left_ref.1, bf16[11,4,256,256]{3,2,1,0:T(8,128)(2,1)} %right_ref.1), custom_call_target="tpu_custom_call" | custom-call | tf_op jit(solution)/shard_map/pallas_call | solution.py:377
  25.6 0.8 %copy.7 = bf16[4,256,256]{2,1,0:T(8,128)(2,1)} copy(bf16[4,256,256]{2,1,0:T(8,128)(2,1)S(1)} %shard_map.55) | data formatting | bytes 1048576

commit v7 on v6

--- a/solution.py
+++ b/solution.py
@@ -57,8 +57,8 @@
     z = lax.div(me, 2)
     c = lax.rem(me, 2)
 
-    def peer(d):
-        return {"op": lax.rem(z + d, nz) * 2 + 1}
+    def peer(d, core):
+        return {"op": lax.rem(z + d, nz) * 2 + core}
 
     sibling = {"op": z * 2 + 1 - c}
     far = sorted(range(1, nz), key=lambda d: -min(d, nz - d))
@@ -104,18 +104,16 @@
     def _():
         signal(barrier, beside(1, 1))
 
-    signal(barrier, sibling)
-
-    @pl.when(c == 1)
-    def _():
-        for d in far:
-            signal(barrier, {"op": lax.rem(z + d, nz) * 2})
-
     load_dims = pltpu.make_async_copy(dims_hbm, dims_ref, small_sem.at[0])
     load_shift = pltpu.make_async_copy(shift_hbm, shift_ref, small_sem.at[1])
     load_dims.start()
     for s in (3, 0, 1, 2):
         load_wave(s).start()
+    signal(barrier, sibling)
+
+    for d in far:
+        signal(barrier, peer(d, 0))
+
     load_shift.start()
     for copy in load(0):
         copy.start()
@@ -130,9 +128,8 @@
         wide[s + 1] = masked(wide[s + 1].astype(jnp.float32), s, 0)
 
     load_dims.wait()
-    for s in (3, 0):
-        load_wave(s).wait()
-        mask(s)
+    load_wave(3).wait()
+    mask(3)
 
     def halo(i):
         return pltpu.make_async_remote_copy(
@@ -147,14 +144,18 @@
     @pl.when(c == 1)
     def _():
         pl.semaphore_wait(barrier, 1 + before + after)
-
-        @pl.when(before == 1)
-        def _():
-            halo(1).start()
+        signal(ready, sibling)
 
         @pl.when(after == 1)
         def _():
             halo(0).start()
+
+    load_wave(0).wait()
+    mask(0)
+
+    @pl.when((c == 1) & (before == 1))
+    def _():
+        halo(1).start()
 
     def passed(slot):
         return pltpu.make_async_remote_copy(
@@ -188,7 +189,7 @@
             dst_ref=landed.at[p, c * (nz - 1) + d - 1],
             send_sem=rs_send.at[p],
             recv_sem=rs_recv.at[p],
-            device_id=peer(d),
+            device_id=peer(d, p),
             device_id_type=MESH,
         )
 
@@ -210,7 +211,7 @@
             dst_ref=done.at[p, z],
             send_sem=ag_send.at[p],
             recv_sem=ag_recv.at[p, d - 1],
-            device_id=peer(d),
+            device_id=peer(d, p),
             device_id_type=MESH,
         )
 
@@ -276,8 +277,7 @@
 
         @pl.when((it == 0) & (c == 0))
         def _():
-            pl.semaphore_wait(barrier, nz)
-            signal(ready, sibling)
+            pl.semaphore_wait(ready, 1)
 
         @pl.when(q == 0)
         def _():
@@ -291,6 +291,11 @@
             part[p] = both
             packed[p] = both.astype(jnp.bfloat16)
 
+            @pl.when((p == 0) & (c == 0))
+            def _():
+                pl.semaphore_wait(barrier, 2 * nz - 1)
+                signal(ready, sibling)
+
             @pl.when((p == 0) & (c == 1))
             def _():
                 pl.semaphore_wait(ready, 1)
@@ -298,7 +303,7 @@
             for d in far:
                 scatter(p, d).start()
 
-            @pl.when(c == 0)
+            @pl.when(c != p)
             def _():
                 hand_over(p).start()
 
@@ -306,10 +311,11 @@
 
     lax.fori_loop(0, 4, step, 0)
 
-    def reduce(p, carry):
+    def reduce(p):
         mine_now = part[p, mine]
         wait_all(landed.at[p], rs_recv.at[p])
-        sums = [landed[p, 2 * (nz - 1)].astype(jnp.float32), mine_now]
+        given = landed[p, 2 * (nz - 1)].astype(jnp.float32)
+        sums = [jnp.where(p == core, mine_now, given) for core in range(2)]
         for d in range(1, nz):
             for core in range(2):
                 sums[core] += landed[p, core * (nz - 1) + d - 1].astype(jnp.float32)
@@ -318,35 +324,31 @@
         for d in far:
             gather(p, d).start()
         share(p, 0).start()
-        return carry
-
-    def pass_on(p, carry):
+
+    def pass_on(p):
         for d in reversed(far):
             gather(p, d).wait_recv()
             share(p, d).start()
-        return carry
 
     def place(p):
         for core in range(2):
             for n in range(nz):
                 out_ref[sector_of(p, core), pl.ds(n * rows, rows)] = done[p, n, core]
 
-    @pl.when(c == 1)
-    def _():
-        lax.fori_loop(0, 2, reduce, 0)
-        lax.fori_loop(0, 2, pass_on, 0)
+    reduce(c)
+    pass_on(c)
 
     def finish(p, carry):
         to_sibling(p).wait_send()
 
-        @pl.when(c == 0)
+        @pl.when(c != p)
         def _():
             wait_all(packed.at[p], rs_send.at[p])
             wait_all(done.at[p], share_recv.at[p])
 
         place(p)
 
-        @pl.when(c == 1)
+        @pl.when(c == p)
         def _():
             wait_all(landed.at[p, pl.ds(0, nz - 1)], rs_send.at[p])
             wait_all(done.at[p, pl.ds(0, nz - 1)], ag_send.at[p])

time: 26.5 us -> 26 us (0.981)
  the two profiles are of different devices: /device:TPU:7 before, /device:TPU:1 now
where the time goes in v7:
time: 26 us; the launch traced here: 25.9 us
  Pallas kernels  25.1 us (97%)
  local copies, waits for them, and re-layouts  0.8 us (3%)
    pallas_call x1, Pallas kernels, body(): pl.pallas_call(functools.partial(kernel, nsec, nz), out_shape=pltpu.VMEM(...  25.1 us
    unnamed x1, local copies, waits for them, and re-layouts  0.8 us

profile of v7, /device:TPU:1, one launch (start us, length us, event | category | flops | bytes accessed | tf_op | source)
XLA Modules:
  0.0 25.9 jit_solution(12232662242000754410)
XLA Ops:
  0.0 25.1 %shard_map.55 = bf16[4,256,256]{2,1,0:T(8,128)(2,1)S(1)} custom-call(s32[2,4]{1,0:T(2,128)} %bitcast.1, s32[11]{0:T(128)} %shift_hbm.1, bf16[4,256,256]{2,1,0:T(8,128)(2,1)} %wave_ref.1, bf16[11,4,256,256]{3,2,1,0:T(8,128)(2,1)} %left_ref.1, bf16[11,4,256,256]{3,2,1,0:T(8,128)(2,1)} %right_ref.1), custom_call_target="tpu_custom_call" | custom-call | tf_op jit(solution)/shard_map/pallas_call | solution.py:379
  25.1 0.8 %copy.7 = bf16[4,256,256]{2,1,0:T(8,128)(2,1)} copy(bf16[4,256,256]{2,1,0:T(8,128)(2,1)S(1)} %shard_map.55) | data formatting | bytes 1048576

commit v8 on v7

--- a/solution.py
+++ b/solution.py
@@ -129,6 +129,8 @@
 
     load_dims.wait()
     load_wave(3).wait()
+    for copy in load(1):
+        copy.start()
     mask(3)
 
     def halo(i):
@@ -257,7 +259,7 @@
 
         @pl.when(it == 0)
         def _():
-            for later in range(1, 4):
+            for later in range(2, 4):
                 for copy in load(later):
                     copy.start()
 

time: 26 us -> 26 us (level)
  no operation moved by 1% of the time
where the time goes in v8:
time: 26 us; the launch traced here: 25.9 us
  Pallas kernels  25.1 us (97%)
  local copies, waits for them, and re-layouts  0.8 us (3%)
    pallas_call x1, Pallas kernels, body(): pl.pallas_call(functools.partial(kernel, nsec, nz), out_shape=pltpu.VMEM(...  25.1 us
    unnamed x1, local copies, waits for them, and re-layouts  0.8 us

profile of v8, /device:TPU:1, one launch (start us, length us, event | category | flops | bytes accessed | tf_op | source)
XLA Modules:
  0.0 25.9 jit_solution(4229798979221236576)
XLA Ops:
  0.0 25.1 %shard_map.55 = bf16[4,256,256]{2,1,0:T(8,128)(2,1)S(1)} custom-call(s32[2,4]{1,0:T(2,128)} %bitcast.1, s32[11]{0:T(128)} %shift_hbm.1, bf16[4,256,256]{2,1,0:T(8,128)(2,1)} %wave_ref.1, bf16[11,4,256,256]{3,2,1,0:T(8,128)(2,1)} %left_ref.1, bf16[11,4,256,256]{3,2,1,0:T(8,128)(2,1)} %right_ref.1), custom_call_target="tpu_custom_call" | custom-call | tf_op jit(solution)/shard_map/pallas_call | solution.py:381
  25.1 0.8 %copy.7 = bf16[4,256,256]{2,1,0:T(8,128)(2,1)} copy(bf16[4,256,256]{2,1,0:T(8,128)(2,1)S(1)} %shard_map.55) | data formatting | bytes 1048576

commit v9 on v8

--- a/solution.py
+++ b/solution.py
@@ -217,6 +217,16 @@
             device_id_type=MESH,
         )
 
+    def gather_part(p, d, k):
+        return pltpu.make_async_remote_copy(
+            src_ref=done.at[p, z, k],
+            dst_ref=done.at[p, z, k],
+            send_sem=ag_send.at[p],
+            recv_sem=ag_recv.at[p, d - 1],
+            device_id=peer(d, p),
+            device_id_type=MESH,
+        )
+
     def share(p, d):
         chunk = lax.rem(z - d + nz, nz)
         return pltpu.make_async_remote_copy(
@@ -323,7 +333,9 @@
                 sums[core] += landed[p, core * (nz - 1) + d - 1].astype(jnp.float32)
         for core in range(2):
             done[p, z, core] = masked(sums[core], sector_of(p, core), z * rows)
-        for d in far:
+            for d in far[:3]:
+                gather_part(p, d, core).start()
+        for d in far[3:]:
             gather(p, d).start()
         share(p, 0).start()
 

time: 26 us -> 26 us (level)
  no operation moved by 1% of the time
where the time goes in v9:
time: 26 us; the launch traced here: 25.9 us
  Pallas kernels  25.1 us (97%)
  local copies, waits for them, and re-layouts  0.8 us (3%)
    pallas_call x1, Pallas kernels, body(): pl.pallas_call(functools.partial(kernel, nsec, nz), out_shape=pltpu.VMEM(...  25.1 us
    unnamed x1, local copies, waits for them, and re-layouts  0.8 us

profile of v9, /device:TPU:1, one launch (start us, length us, event | category | flops | bytes accessed | tf_op | source)
XLA Modules:
  0.0 25.9 jit_solution(17686926876926143664)
XLA Ops:
  0.0 25.1 %shard_map.55 = bf16[4,256,256]{2,1,0:T(8,128)(2,1)S(1)} custom-call(s32[2,4]{1,0:T(2,128)} %bitcast.1, s32[11]{0:T(128)} %shift_hbm.1, bf16[4,256,256]{2,1,0:T(8,128)(2,1)} %wave_ref.1, bf16[11,4,256,256]{3,2,1,0:T(8,128)(2,1)} %left_ref.1, bf16[11,4,256,256]{3,2,1,0:T(8,128)(2,1)} %right_ref.1), custom_call_target="tpu_custom_call" | custom-call | tf_op jit(solution)/shard_map/pallas_call | solution.py:393
  25.2 0.8 %copy.7 = bf16[4,256,256]{2,1,0:T(8,128)(2,1)} copy(bf16[4,256,256]{2,1,0:T(8,128)(2,1)S(1)} %shard_map.55) | data formatting | bytes 1048576
